TPU v7x, 32 devices: a whole 2x2x4 slice. The times are simulated.
32 devices in a mesh: groups: 2 (over y), vocab: 4 (over z), tokens: 2 (over x), sub: 2 (over core).
Axes of the slice: x: 2, y: 2, z: 4, core: 2. Of those that a mesh axis runs over, the one named last changes fastest.
Arguments:
- student_hidden: bfloat16 [256, 4096], P(('groups', 'tokens', 'sub'), 'vocab'), parts along dimension 0, may hold values from -32 to 32
- teacher_hidden: bfloat16 [512, 4096], P(('groups', 'tokens', 'sub'), 'vocab'), parts along dimension 0, may hold values from -32 to 32
- student_head: bfloat16 [4992, 4096], P(('vocab', 'tokens', 'sub')), may hold values from -0.28125 to 0.28125
- teacher_head: bfloat16 [4992, 4096], P(('vocab', 'tokens', 'sub')), may hold values from -0.28125 to 0.28125
- token_ids: int32 [256], P('groups'), parts along dimension 0, may hold values from 0 to 4991
- requests: int32 [8, 4, 16], P('groups'), parts along dimension 0, may hold values from 0 to 63, as said below
- counts: int32 [8, 4], P('groups'), parts along dimension 0, may hold values from 0 to 16, as said below
- kl_weights: float32 [256], P('groups'), parts along dimension 0, may hold values from 0.5 to 2
Outputs:
- grad_hidden: float32 [256, 4096], P(('groups', 'tokens', 'sub'), 'vocab'), parts along dimension 0
- kl: float32 [256], P(('groups', 'tokens', 'sub')), parts along dimension 0
- log_ratio: float32 [256], P(('groups', 'tokens', 'sub')), parts along dimension 0
There are 2 independent parts, one for each index of `groups`. A program takes and returns all parts, laid end to end along the dimension named above; an argument that names none is the same for every part. Nothing has to cross between parts.
Inputs may be any that keep to these rules, and one draw needn't show every extreme that they name: `counts`: row o lists how many of owner o's 32 rows each serving shard supplies, in shard order; each row sums to 32, and in each row one shard supplies exactly 16. requests[o, j, k] for k < counts[o, j] is a row local to serving shard j; over all owners no row of a shard is requested twice; later slots hold valid rows that are not used.
All inputs are finite; a program needn't handle non-finite values.
Results may differ from a plain program's by a relative error of at most 0.012.
Values may be sent and summed in bfloat16 or wider, within the bound.
A program may use at most 64 MiB of HBM per device.

v0:
```python
import jax
import jax.numpy as jnp
from jax import lax
from jax.sharding import PartitionSpec as P


def owner_layout(counts, row_count):
    starts = jnp.cumsum(counts, axis=1) - counts
    within = jnp.arange(row_count, dtype=jnp.int32)
    source = jnp.sum((starts[:, None, :] <= within[None, :, None]).astype(jnp.int32), axis=2) - 1
    slot_index = within[None, :] - jnp.take_along_axis(starts, source, axis=1)
    return (source, slot_index)


def on_device(
    student_hidden,
    teacher_hidden,
    student_head,
    teacher_head,
    token_ids,
    requests,
    counts,
    kl_weights,
):
    owners = lax.axis_size(("tokens", "sub"))
    owner_index = lax.axis_index(("tokens", "sub"))
    row_count = student_hidden.shape[0]
    span_width = student_hidden.shape[1]
    capacity = requests.shape[2]
    source, slot_index = owner_layout(counts, row_count)
    wanted = lax.dynamic_index_in_dim(requests, owner_index, axis=1, keepdims=False)
    outgoing = jnp.take(teacher_hidden, wanted.reshape(-1), axis=0)
    arrived = lax.all_to_all(
        outgoing.reshape(owners, capacity, span_width),
        ("tokens", "sub"),
        split_axis=0,
        concat_axis=0,
        tiled=True,
    )
    my_source = lax.dynamic_index_in_dim(source, owner_index, axis=0, keepdims=False)
    my_slot = lax.dynamic_index_in_dim(slot_index, owner_index, axis=0, keepdims=False)
    teacher_mine = jnp.take(
        arrived.reshape(owners * capacity, span_width), my_source * capacity + my_slot, axis=0
    )
    student_rows, teacher_rows = (
        lax.all_gather(student_hidden, ("tokens", "sub"), axis=0, tiled=True),
        lax.all_gather(teacher_mine, ("tokens", "sub"), axis=0, tiled=True),
    )
    columns = student_head.shape[0]
    contract = (((1,), (1,)), ((), ()))
    student_part = lax.dot_general(
        student_head,
        lax.all_gather(student_rows, "vocab", axis=1, tiled=True),
        contract,
        preferred_element_type=jnp.float32,
    )
    teacher_part = lax.dot_general(
        teacher_head,
        lax.all_gather(teacher_rows, "vocab", axis=1, tiled=True),
        contract,
        preferred_element_type=jnp.float32,
    )
    block_index = lax.axis_index(("vocab", "tokens", "sub"))
    vocab_ids = block_index * columns + jnp.arange(columns, dtype=jnp.int32)
    picked = (vocab_ids[:, None] == token_ids[None, :]).astype(jnp.float32)
    student_hit = jnp.sum(picked * student_part, axis=0)
    teacher_hit = jnp.sum(picked * teacher_part, axis=0)
    difference = student_part - teacher_part
    student_top, teacher_top = lax.pmax(
        (jnp.max(student_part, axis=0), jnp.max(teacher_part, axis=0)), ("vocab", "tokens", "sub")
    )
    student_exp = jnp.exp(student_part - student_top)
    teacher_local = jnp.sum(jnp.exp(teacher_part - teacher_top), axis=0)
    student_total, teacher_total, cross_sum, student_hit, teacher_hit = lax.psum(
        (
            jnp.sum(student_exp, axis=0),
            teacher_local,
            jnp.sum(student_exp * difference, axis=0),
            student_hit,
            teacher_hit,
        ),
        ("vocab", "tokens", "sub"),
    )
    student_norm = student_top + jnp.log(student_total)
    teacher_norm = teacher_top + jnp.log(teacher_total)
    kl_full = cross_sum / student_total - student_norm + teacher_norm
    ratio_full = student_hit - student_norm - (teacher_hit - teacher_norm)
    gap = difference - student_norm + teacher_norm
    dlogits = (
        kl_weights[None, :] * (student_exp / student_total) * (gap - kl_full[None, :])
    ).astype(jnp.bfloat16)
    across = (((0,), (0,)), ((), ()))
    feature_part = lax.psum_scatter(
        lax.dot_general(student_head, dlogits, across, preferred_element_type=jnp.float32).astype(
            jnp.bfloat16
        ),
        "vocab",
        scatter_dimension=0,
        tiled=True,
    )
    grad_hidden = (
        lax.psum_scatter(feature_part, ("tokens", "sub"), scatter_dimension=1, tiled=True)
        .astype(jnp.float32)
        .T
    )
    kl = lax.dynamic_slice_in_dim(kl_full, owner_index * row_count, row_count)
    log_ratio = lax.dynamic_slice_in_dim(ratio_full, owner_index * row_count, row_count)
    return (grad_hidden, kl, log_ratio)


def solution(mesh):
    placed = (
        P(("groups", "tokens", "sub"), "vocab"),
        P(("groups", "tokens", "sub"), "vocab"),
        P(("vocab", "tokens", "sub"), None),
        P(("vocab", "tokens", "sub"), None),
        P("groups"),
        P("groups", None, None),
        P("groups", None),
        P("groups"),
    )
    return jax.shard_map(
        on_device,
        mesh=mesh,
        in_specs=placed,
        out_specs=(
            P(("groups", "tokens", "sub"), "vocab"),
            P(("groups", "tokens", "sub")),
            P(("groups", "tokens", "sub")),
        ),
        check_vma=False,
    )
```

profile of v0, /device:TPU:0, one launch (start us, length us, event | category | flops | bytes accessed | tf_op | source)
XLA Modules:
  0.0 193.7 jit_solution(14660221219864230724)
XLA Ops:
  7.2 0.0 copy-start
  7.2 0.0 all-gather.3.cloned.1.call-start
  7.2 8.9 %all_gather.12 = bf16[128,1024]{1,0:T(8,128)(2,1)} all-gather(bf16[32,1024]{1,0:T(8,128)(2,1)} %param.8), channel_id=1, replica_groups=mesh['groups'=2,'vocab'=4,'tokens'=2,'sub'=2] {'tokens','sub'}, dimensions={0}, use_global_device_ids=true | all-gather | bytes 327680 | tf_op jit(solution)/shard_map/all_gather | solution.py:46
  16.2 0.0 all-gather.3.cloned.1.call-update
  16.2 0.5 broadcast.163
  16.7 1.4 fusion.20
  18.1 0.1 reshape.140
  18.2 1.7 gather_fusion
  19.9 0.7 broadcast_select_fusion
  20.6 3.3 %all-to-all-start = ((bf16[4,16,1024]{2,1,0:T(8,128)(2,1)}), bf16[4,16,1024]{2,1,0:T(8,128)(2,1)S(1)}, u32[]{:S(2)}, u32[]{:S(2)}) async-start(bf16[4,16,1024]{2,1,0:T(8,128)(2,1)} %broadcast_select_fusion), calls=%async_computation | async-start | bytes 262144 | tf_op jit(solution)/shard_map/all_to_all | solution.py:33
  24.0 0.0 all-gather.5.cloned.1.call-start
  24.0 0.9 reduce_window_sum.11
  24.9 0.7 sub.66
  25.6 0.1 convert_reduce_fusion
  25.7 0.1 reshape.158
  25.8 1.5 gather_fusion.2
  27.3 0.1 reshape.161
  27.4 1.2 all-to-all-done
  28.6 0.6 gather_fusion.1
  29.2 0.1 broadcast_select_fusion.1
  29.3 6.2 %all_gather.14 = bf16[128,1024]{1,0:T(8,128)(2,1)} all-gather(bf16[32,1024]{1,0:T(8,128)(2,1)S(1)} %broadcast_select_fusion.1), channel_id=1, replica_groups=mesh['groups'=2,'vocab'=4,'tokens'=2,'sub'=2] {'tokens','sub'}, dimensions={0}, use_global_device_ids=true | all-gather | bytes 327680 | tf_op jit(solution)/shard_map/all_gather | solution.py:47
  35.5 0.0 all-gather.5.cloned.1.call-update
  35.5 0.0 reduce-scatter.3.cloned.1.call-start
  35.6 9.0 %all-gather.3.cloned.1.call-done = bf16[128,4096]{1,0:T(8,128)(2,1)} async-done(((bf16[128,1024]{1,0:T(8,128)(2,1)}), bf16[128,4096]{1,0:T(8,128)(2,1)}) %all-gather.3.cloned.1.call-update) | async-done | bytes 1048592 | tf_op jit(solution)/shard_map/all_gather | solution.py:53
  44.6 0.0 copy-done
  44.6 2.1 %fusion.22 = (f32[128]{0:T(128)S(1)}, f32[312,128]{1,0:T(8,128)S(1)}) fusion(bf16[312,4096]{1,0:T(8,128)(2,1)S(1)} %copy-done, bf16[128,4096]{1,0:T(8,128)(2,1)} %all-gather.3.cloned.1.call-done), kind=kOutput, calls=%fused_computation.57 | convolution fusion | flops 327195520 | bytes 3764736 | tf_op jit(solution)/shard_map/dot_general | solution.py:51
  46.7 0.0 copy-start.1
  46.7 0.0 copy-start.2
  46.7 26.9 %all-gather.5.cloned.1.call-done = bf16[128,4096]{1,0:T(8,128)(2,1)} async-done(((bf16[128,1024]{1,0:T(8,128)(2,1)}), bf16[128,4096]{1,0:T(8,128)(2,1)}) %all-gather.5.cloned.1.call-update) | async-done | bytes 1048592 | tf_op jit(solution)/shard_map/all_gather | solution.py:59
  73.7 2.9 %fusion.21 = (f32[128]{0:T(128)S(1)}, f32[128,312]{0,1:T(8,128)S(1)}) fusion(bf16[128,4096]{1,0:T(8,128)(2,1)} %all-gather.5.cloned.1.call-done, bf16[312,4096]{1,0:T(8,128)(2,1)} %param.11), kind=kOutput, calls=%fused_computation.56 | convolution fusion | flops 327195520 | bytes 3764736 | tf_op jit(solution)/shard_map/dot_general | solution.py:57
  76.6 31.9 %all-reduce.1 = (f32[128]{0:T(128)S(1)}, f32[128]{0:T(128)S(1)}) all-reduce(f32[128]{0:T(128)S(1)} %get-tuple-element.24, f32[128]{0:T(128)S(1)} %get-tuple-element.26), channel_id=1, replica_groups=mesh['groups'=2,'vocab'=4,'tokens'=2,'sub'=2] {'vocab','tokens','sub'}, use_global_device_ids=true, to_apply=%region_7.8 | all-reduce | flops 256 | bytes 2048 | tf_op jit(solution)/shard_map/pmax | solution.py:69
  108.5 0.0 copy-done.1
  108.5 0.1 multiply_reduce_fusion
  108.6 29.5 %all-reduce = (f32[128]{0:T(128)S(1)}, f32[128]{0:T(128)S(1)}, f32[128]{0:T(128)S(1)}, f32[128]{0:T(128)S(1)}, f32[128]{0:T(128)S(1)}) all-reduce(f32[128]{0:T(128)S(1)} %get-tuple-element.7, f32[128]{0:T(128)S(1)} %get-tuple-element.4, ...), channel_id=1, replica_groups=mesh['groups'=2,'vocab'=4,'tokens'=2,'sub'=2] {'vocab','tokens','sub'}, use_global_device_ids=true, to_apply=%region_9.10 | all-reduce | flops 640 | bytes 5120 | tf_op jit(solution)/shard_map/psum | solution.py:74
  138.1 0.0 copy-done.2
  138.1 1.8 fusion
  140.0 0.0 reduce-scatter.3.cloned.1.call-update
  140.0 0.0 reduce-scatter.5.cloned.1.call-start
  140.0 24.5 %reduce-scatter.3.cloned.1.call-done = bf16[1024,128]{0,1:T(8,128)(2,1)} async-done(((bf16[4096,128]{0,1:T(8,128)(2,1)}), bf16[1024,128]{0,1:T(8,128)(2,1)}) %reduce-scatter.3.cloned.1.call-update) | async-done | bytes 262160 | tf_op jit(solution)/shard_map/reduce_scatter | solution.py:93
  164.5 0.0 reduce-scatter.5.cloned.1.call-update
  164.5 0.6 dynamic_slice.20
  165.1 0.6 dynamic_slice.21
  165.7 20.0 %reduce-scatter.5.cloned.1.call-done = bf16[1024,32]{0,1:T(8,128)(2,1)} async-done(((bf16[1024,128]{0,1:T(8,128)(2,1)}), bf16[1024,32]{0,1:T(8,128)(2,1)}) %reduce-scatter.5.cloned.1.call-update) | async-done | bytes 65552 | tf_op jit(solution)/shard_map/reduce_scatter | solution.py:102
  185.7 1.5 convert_bitcast_fusion
  (11 shorter events, 0.1 us)
Async XLA Ops:
  7.2 37.5 %copy-start = (bf16[312,4096]{1,0:T(8,128)(2,1)S(1)}, bf16[312,4096]{1,0:T(8,128)(2,1)}, u32[]{:S(2)}) copy-start(bf16[312,4096]{1,0:T(8,128)(2,1)} %param.10) | copy-start | bytes 7667716
  7.2 37.5 %all-gather.3.cloned.1.call-start = ((), (), s32[]{:S(2)}) async-start(), calls=%async_computation.3 | async-start | bytes 1310720 | tf_op jit(solution)/shard_map/all_gather | solution.py:53
  20.6 7.9 %all-to-all-start = ((bf16[4,16,1024]{2,1,0:T(8,128)(2,1)}), bf16[4,16,1024]{2,1,0:T(8,128)(2,1)S(1)}, u32[]{:S(2)}, u32[]{:S(2)}) async-start(bf16[4,16,1024]{2,1,0:T(8,128)(2,1)} %broadcast_select_fusion), calls=%async_computation | async-start | bytes 262144 | tf_op jit(solution)/shard_map/all_to_all | solution.py:33
  24.0 49.7 %all-gather.5.cloned.1.call-start = ((), (), s32[]{:S(2)}) async-start(), calls=%async_computation.4 | async-start | bytes 1310720 | tf_op jit(solution)/shard_map/all_gather | solution.py:59
  35.5 129.0 %reduce-scatter.3.cloned.1.call-start = ((), (), s32[]{:S(2)}) async-start(), calls=%async_computation.5 | async-start | bytes 1310720 | tf_op jit(solution)/shard_map/reduce_scatter | solution.py:93
  46.7 61.7 %copy-start.1 = (s32[128]{0:T(128)S(1)}, s32[128]{0:T(128)}, u32[]{:S(2)}) copy-start(s32[128]{0:T(128)} %param.12) | copy-start | bytes 1540
  46.7 91.4 %copy-start.2 = (f32[128]{0:T(128)S(1)}, f32[128]{0:T(128)}, u32[]{:S(2)}) copy-start(f32[128]{0:T(128)} %param.15) | copy-start | bytes 1540
  140.0 45.7 %reduce-scatter.5.cloned.1.call-start = ((), (), s32[]{:S(2)}) async-start(), calls=%async_computation.6 | async-start | bytes 327680 | tf_op jit(solution)/shard_map/reduce_scatter | solution.py:102
Sparse Core Ops, SparseCore 0:
  16.3 28.2 all-gather.2
  46.2 27.4 all-gather.4
  140.1 24.3 reduce-scatter.2
  167.0 18.6 reduce-scatter.4
where the time goes:
time: 194 us
  waiting for transfers between devices  81.6 us (42%)
  blocking collectives  76.5 us (39%)
  between operations  13.9 us (7%)
  local copies, waits for them, and re-layouts  7.19 us (4%)
  matrix products  6.82 us (4%)
  other arithmetic  4.17 us (2%)
  starting transfers between devices  3.49 us (2%)
    pmax x1, blocking collectives, on_device(): lax.pmax((jnp.max(student_part, axis=0), jnp.max(teacher_part, axis=0)),...  31.9 us
    psum x1, blocking collectives, on_device(): lax.psum((jnp.sum(student_exp, axis=0), teacher_local, jnp.sum(student_ex...  29.5 us
    all_gather x1, waiting for transfers between devices, on_device(): lax.all_gather(teacher_rows, 'vocab', axis=1, tiled=True)  26.9 us
    reduce_scatter x1, waiting for transfers between devices, on_device(): lax.psum_scatter(lax.dot_general(student_head, dlogits, across, preferred...  24.5 us
    reduce_scatter x1, waiting for transfers between devices, on_device(): lax.psum_scatter(feature_part, ('tokens', 'sub'), scatter_dimension=1, ti...  20 us
    all_gather x1, waiting for transfers between devices, on_device(): lax.all_gather(student_rows, 'vocab', axis=1, tiled=True)  9.04 us
    all_gather x1, blocking collectives, on_device(): lax.all_gather(student_hidden, ('tokens', 'sub'), axis=0, tiled=True)  8.93 us
    all_gather x1, blocking collectives, on_device(): lax.all_gather(teacher_mine, ('tokens', 'sub'), axis=0, tiled=True)  6.22 us
  transfers between devices with their start and end apart: 5, of which 5 were waited for; matrix products, arithmetic and copies ran while one was open for 6% of the time, Pallas kernels for 0%

commit v1 on v0

v1 whole, which is shorter than its diff:
```python
import functools

import jax
import jax.numpy as jnp
from jax import lax
from jax.experimental import pallas as pl
from jax.experimental.pallas import tpu as pltpu
from jax.sharding import PartitionSpec as P

MESH = pl.DeviceIdType.MESH
F32 = jnp.float32
BF16 = jnp.bfloat16


def kernel(
    spans, tiles, cores,
    counts_ref, student_ref, teacher_ref, student_head, teacher_head, token_ref, request_ref, weight_ref,
    grad_ref, row_ref,
    heads, hidden, slots, arrived, logits, stats, terms, core_in, core_out, tile_in, tile_out, span_in, span_out,
    head_sem, slot_send, slot_recv, span_send, tile_send, core_send, span_recv, tile_recv, core_recv,
    stat_send, stat_recv, gcore_send, gcore_recv, gtile_send, gtile_recv, gspan_send, gspan_recv,
):
    group = lax.axis_index("groups")
    v = lax.axis_index("vocab")
    t = lax.axis_index("tokens")
    s = lax.axis_index("sub")
    owners = tiles * cores
    members = spans * owners
    owner = t * cores + s
    me = v * owners + owner
    rows, width = student_ref.shape
    columns = student_head.shape[0]
    capacity = request_ref.shape[1] // owners

    def remote(src, dst, send, recv, at):
        copy = pltpu.make_async_remote_copy(
            src_ref=src, dst_ref=dst, send_sem=send, recv_sem=recv,
            device_id=(group,) + tuple(at), device_id_type=MESH,
        )
        copy.start()

    def drain(ref, sem):
        pltpu.make_async_copy(ref, ref, sem).wait()

    def member(index):
        return (index // owners, (index % owners) // cores, index % cores)

    def around(i):
        return lax.rem(me + i, members)

    @pl.loop(1, members)
    def _(i):
        pl.semaphore_signal(
            pltpu.get_barrier_semaphore(), inc=1, device_id=(group,) + member(around(i)), device_id_type=MESH
        )

    head_copies = [
        pltpu.make_async_copy(ref, heads.at[which], head_sem.at[which])
        for which, ref in enumerate((student_head, teacher_head))
    ]
    for copy in head_copies:
        copy.start()

    served = teacher_ref.shape[0]
    wanted = request_ref[pl.ds(owner, 1), :]
    pick = (lax.broadcasted_iota(jnp.int32, (served, owners * capacity), 0) == wanted).astype(F32).astype(BF16)
    slots[...] = (
        lax.dot_general(pick, teacher_ref[...], (((0,), (0,)), ((), ())), preferred_element_type=F32)
        .astype(BF16)
        .reshape(owners, capacity, width)
    )
    arrived[owner] = slots[owner]
    hidden[0, v, t, s] = student_ref[...]

    pl.semaphore_wait(pltpu.get_barrier_semaphore(), members - 1)

    for i in range(1, owners):
        other = lax.rem(owner + i, owners)
        remote(slots.at[other], arrived.at[owner], slot_send, slot_recv, (v, other // cores, lax.rem(other, cores)))

    def to_tiles(a, w):
        for i in range(1, tiles):
            remote(hidden.at[a, w, t, s], hidden.at[a, w, t, s], tile_send.at[a], tile_recv.at[a, w],
                   (v, lax.rem(t + i, tiles), s))

    def to_core(a, w, u):
        for i in range(1, cores):
            remote(hidden.at[a, w, u, s], hidden.at[a, w, u, s], core_send.at[a], core_recv.at[a, w],
                   (v, t, lax.rem(s + i, cores)))

    def to_spans(a):
        for d in range(1, spans):
            remote(hidden.at[a, v, t, s], hidden.at[a, v, t, s], span_send.at[a], span_recv.at[a, v],
                   (lax.rem(v + spans - d, spans), t, s))

    def start_own(a):
        to_spans(a)
        to_tiles(a, v)
        to_core(a, v, t)

    def take_teacher():
        drain(arrived.at[pl.ds(0, owners - 1)], slot_recv)
        line = lax.broadcasted_iota(jnp.int32, (rows, owners * capacity), 0)
        lane = lax.broadcasted_iota(jnp.int32, (rows, owners * capacity), 1)
        chosen = jnp.zeros((rows, owners * capacity), jnp.int32)
        start = jnp.int32(0)
        for j in range(owners):
            count = counts_ref[owner, j]
            place = lane - j * capacity
            hit = (place >= 0) & (place < count) & (place + start == line)
            chosen = jnp.where(hit, 1, chosen)
            start = start + count
        mine = jnp.dot(
            chosen.astype(F32).astype(BF16),
            arrived[...].reshape(owners * capacity, width),
            preferred_element_type=F32,
        )
        hidden[1, v, t, s] = mine.astype(BF16)
        start_own(1)

    def span_step(a, d):
        if d == 0:
            return
        w = lax.rem(v + d, spans)
        drain(hidden.at[a, w, t, s], span_recv.at[a, w])
        to_tiles(a, w)
        to_core(a, w, t)

    def tile_step(a, d):
        w = lax.rem(v + d, spans)
        if tiles > 1:
            drain(hidden.at[a, w, pl.ds(0, tiles - 1), 0], tile_recv.at[a, w])
        for i in range(1, tiles):
            to_core(a, w, lax.rem(t + i, tiles))

    def core_step(a, d):
        w = lax.rem(v + d, spans)
        if cores > 1:
            drain(hidden.at[a, w, :, pl.ds(0, cores - 1)], core_recv.at[a, w])
        if d == 0:
            head_copies[a].wait()
        part = lax.dot_general(
            heads[a, :, pl.ds(pl.multiple_of(w * width, width), width)],
            hidden[a, w].reshape(owners * rows, width),
            (((1,), (1,)), ((), ())),
            preferred_element_type=F32,
        )
        logits[a] = part if d == 0 else logits[a] + part

    start_own(0)
    units = [(0, 0)]
    for d in range(spans):
        if d + 1 < spans:
            units.append((0, d + 1))
        units.append((1, d))
    for i in range(len(units) + 2):
        if i < len(units):
            if units[i] == (1, 0):
                take_teacher()
            span_step(*units[i])
        if 0 <= i - 1 < len(units):
            tile_step(*units[i - 1])
        if 0 <= i - 2:
            core_step(*units[i - 2])

    student, teacher = logits[0], logits[1]
    ids = me * columns + lax.broadcasted_iota(jnp.int32, student.shape, 0)
    here = ids == token_ref[...]
    gap = student - teacher
    student_top = jnp.max(student, axis=0, keepdims=True)
    teacher_top = jnp.max(teacher, axis=0, keepdims=True)
    student_exp = jnp.exp(student - student_top)
    parts = [
        student_top,
        teacher_top,
        jnp.sum(student_exp, axis=0, keepdims=True),
        jnp.sum(jnp.exp(teacher - teacher_top), axis=0, keepdims=True),
        jnp.sum(student_exp * gap, axis=0, keepdims=True),
        jnp.sum(jnp.where(here, gap, 0.0), axis=0, keepdims=True),
    ]
    parts += [jnp.zeros_like(student_top)] * 2
    stats[me] = jnp.concatenate(parts, axis=0)

    @pl.loop(1, members)
    def _(i):
        remote(stats.at[me], stats.at[me], stat_send, stat_recv, member(around(i)))

    drain(stats.at[pl.ds(0, members - 1)], stat_recv)
    every = stats[...]
    student_tops, teacher_tops = every[:, 0, :], every[:, 1, :]
    top_s = jnp.max(student_tops, axis=0, keepdims=True)
    top_t = jnp.max(teacher_tops, axis=0, keepdims=True)
    scale_s = jnp.exp(student_tops - top_s)
    scale_t = jnp.exp(teacher_tops - top_t)
    total_s = jnp.sum(scale_s * every[:, 2, :], axis=0, keepdims=True)
    total_t = jnp.sum(scale_t * every[:, 3, :], axis=0, keepdims=True)
    cross = jnp.sum(scale_s * every[:, 4, :], axis=0, keepdims=True)
    hit = jnp.sum(every[:, 5, :], axis=0, keepdims=True)
    norm_s = top_s + jnp.log(total_s)
    norm_t = top_t + jnp.log(total_t)
    shift = norm_t - norm_s
    kl = cross / total_s + shift
    ratio = hit + shift
    prob = jnp.exp(logits[0] - norm_s)
    slope = (weight_ref[...] * prob * (logits[0] - logits[1] + shift - kl)).astype(BF16)

    def grad_block(d):
        w = lax.rem(v + d, spans)
        term = lax.dot_general(
            slope,
            heads[0, :, pl.ds(pl.multiple_of(w * width, width), width)],
            (((0,), (0,)), ((), ())),
            preferred_element_type=F32,
        )
        terms[d] = term.reshape(tiles, cores, rows, width)
        core_out[d] = term.astype(BF16).reshape(tiles, cores, rows, width)
        for i in range(1, cores):
            peer = lax.rem(s + i, cores)
            for u in range(tiles):
                remote(core_out.at[d, u, peer], core_in.at[d, s, u], gcore_send, gcore_recv.at[d], (v, t, peer))

    def grad_core(d):
        drain(core_in.at[d, pl.ds(0, cores - 1)], gcore_recv.at[d])
        for i in range(1, tiles + 1):
            u = lax.rem(t + i, tiles)
            total = terms[d, u, s]
            for j in range(1, cores):
                total = total + core_in[d, lax.rem(s + j, cores), u].astype(F32)
            if i < tiles:
                tile_out[d, u] = total.astype(BF16)
                remote(tile_out.at[d, u], tile_in.at[d, t], gtile_send, gtile_recv.at[d], (v, u, s))
            else:
                terms[d, u, s] = total

    def grad_tile(d):
        if tiles > 1:
            drain(tile_in.at[d, pl.ds(0, tiles - 1)], gtile_recv.at[d])
        total = terms[d, t, s]
        for i in range(1, tiles):
            total = total + tile_in[d, lax.rem(t + i, tiles)].astype(F32)
        if d == 0:
            grad_ref[...] = total
        else:
            span_out[d] = total.astype(BF16)
            remote(span_out.at[d], span_in.at[d], gspan_send, gspan_recv, (lax.rem(v + d, spans), t, s))

    order = list(range(1, spans)) + [0]
    for i in range(len(order) + 2):
        if i < len(order):
            grad_block(order[i])
        if 0 <= i - 1 < len(order):
            grad_core(order[i - 1])
        if 0 <= i - 2:
            grad_tile(order[i - 2])

    turn = lax.rem(owners - owner, owners) * rows
    row_ref[...] = pltpu.roll(
        jnp.concatenate([kl, ratio] + [jnp.zeros_like(kl)] * 6, axis=0), turn, axis=1
    )

    total = grad_ref[...]
    drain(span_in.at[pl.ds(1, spans - 1)], gspan_recv)
    for d in range(1, spans):
        total = total + span_in[d].astype(F32)
    grad_ref[...] = total

    drain(slots.at[pl.ds(0, owners - 1)], slot_send)
    for a in range(2):
        drain(hidden.at[a, pl.ds(0, spans - 1), 0, 0], span_send.at[a])
        if tiles > 1:
            drain(hidden.at[a, :, pl.ds(0, tiles - 1), 0], tile_send.at[a])
        drain(hidden.at[a, :, :, pl.ds(0, cores - 1)], core_send.at[a])
    drain(stats.at[pl.ds(0, members - 1)], stat_send)
    drain(core_out.at[:, :, pl.ds(0, cores - 1)], gcore_send)
    if tiles > 1:
        drain(tile_out.at[:, pl.ds(0, tiles - 1)], gtile_send)
    drain(span_out.at[pl.ds(1, spans - 1)], gspan_send)


def on_device(mesh, student_hidden, teacher_hidden, student_head, teacher_head, token_ids, requests, counts, kl_weights):
    spans, tiles, cores = (mesh.shape[name] for name in ("vocab", "tokens", "sub"))
    owners = tiles * cores
    members = spans * owners
    rows, width = student_hidden.shape
    columns, features = student_head.shape
    capacity = requests.shape[2]
    total_rows = owners * rows
    vmem = pl.BlockSpec(memory_space=pltpu.VMEM)
    dma = pltpu.SemaphoreType.DMA
    grad, row_values = pl.pallas_call(
        functools.partial(kernel, spans, tiles, cores),
        out_shape=(
            jax.ShapeDtypeStruct((rows, width), F32),
            jax.ShapeDtypeStruct((8, total_rows), F32),
        ),
        in_specs=[
            pl.BlockSpec(memory_space=pltpu.SMEM), vmem, vmem,
            pl.BlockSpec(memory_space=pl.ANY), pl.BlockSpec(memory_space=pl.ANY), vmem, vmem, vmem,
        ],
        out_specs=(vmem, vmem),
        scratch_shapes=[
            pltpu.VMEM((2, columns, features), BF16),
            pltpu.VMEM((2, spans, tiles, cores, rows, width), BF16),
            pltpu.VMEM((owners, capacity, width), BF16),
            pltpu.VMEM((owners, capacity, width), BF16),
            pltpu.VMEM((2, columns, total_rows), F32),
            pltpu.VMEM((members, 8, total_rows), F32),
            pltpu.VMEM((spans, tiles, cores, rows, width), F32),
            pltpu.VMEM((spans, cores, tiles, rows, width), BF16),
            pltpu.VMEM((spans, tiles, cores, rows, width), BF16),
            pltpu.VMEM((spans, tiles, rows, width), BF16),
            pltpu.VMEM((spans, tiles, rows, width), BF16),
            pltpu.VMEM((spans, rows, width), BF16),
            pltpu.VMEM((spans, rows, width), BF16),
            dma((2,)), dma, dma, dma((2,)), dma((2,)), dma((2,)),
            dma((2, spans)), dma((2, spans)), dma((2, spans)),
            dma, dma, dma, dma((spans,)), dma, dma((spans,)), dma, dma,
        ],
        compiler_params=pltpu.CompilerParams(
            collective_id=0, has_side_effects=True, vmem_limit_bytes=56 * 1024 * 1024
        ),
    )(
        counts, student_hidden, teacher_hidden, student_head, teacher_head,
        token_ids.reshape(1, total_rows),
        requests.transpose(1, 0, 2).reshape(owners, owners * capacity),
        kl_weights.reshape(1, total_rows),
    )
    return grad, row_values[0, :rows], row_values[1, :rows]


def solution(mesh):
    placed = (
        P(("groups", "tokens", "sub"), "vocab"),
        P(("groups", "tokens", "sub"), "vocab"),
        P(("vocab", "tokens", "sub"), None),
        P(("vocab", "tokens", "sub"), None),
        P("groups"),
        P("groups", None, None),
        P("groups", None),
        P("groups"),
    )
    return jax.shard_map(
        functools.partial(on_device, mesh),
        mesh=mesh,
        in_specs=placed,
        out_specs=(
            P(("groups", "tokens", "sub"), "vocab"),
            P(("groups", "tokens", "sub")),
            P(("groups", "tokens", "sub")),
        ),
        check_vma=False,
    )
```

time: 194 us -> 51.4 us (0.26)
  waiting for transfers between devices: 81.6 us -> 0 us
  blocking collectives: 76.5 us -> 0 us
  Pallas kernels: 0 us -> 46.3 us
  between operations: 13.9 us -> 0.64 us
  matrix products: 6.82 us -> 0 us
  other arithmetic: 4.17 us -> 0 us
  starting transfers between devices: 3.49 us -> 0 us
  local copies, waits for them, and re-layouts: 7.19 us -> 4.2 us
    pallas_call x0 -> x1, Pallas kernels: none -> 46.3 us  [on_device(): pl.pallas_call(functools.partial(kernel, spans, tiles, cores), out_shape=...]
    reduce_scatter x2 -> x0, waiting for transfers between devices: 44.4 us -> none  [the longest x1 24.5 us: on_device(): lax.psum_scatter(lax.dot_general(student_head, dlogits, across, preferred...]
    all_gather x2 -> x0, waiting for transfers between devices: 36 us -> none  [the longest x1 26.9 us: on_device(): lax.all_gather(teacher_rows, 'vocab', axis=1, tiled=True)]
    pmax x1 -> x0, blocking collectives: 31.9 us -> none  [on_device(): lax.pmax((jnp.max(student_part, axis=0), jnp.max(teacher_part, axis=0)),...]
    psum x1 -> x0, blocking collectives: 29.5 us -> none  [on_device(): lax.psum((jnp.sum(student_exp, axis=0), teacher_local, jnp.sum(student_ex...]
    all_gather x2 -> x0, blocking collectives: 15.2 us -> none  [the longest x1 8.93 us: on_device(): lax.all_gather(student_hidden, ('tokens', 'sub'), axis=0, tiled=True)]
    dot_general x3 -> x0, matrix products: 6.82 us -> none  [the longest x1 2.9 us: on_device(): lax.dot_general(teacher_head, lax.all_gather(teacher_rows, 'vocab', axis=...]
    gather x5 -> x0, local copies, waits for them, and re-layouts: 4.03 us -> none  [the longest x1 1.72 us: on_device(): outgoing = jnp.take(teacher_hidden, wanted.reshape(-1), axis=0)]
  transfers between devices with their start and end apart: 5 -> 0, of which waited for: 5 -> 0; matrix products, arithmetic and copies ran while one was open for 6% -> 0% of each run, Pallas kernels for 0% -> 0%
where the time goes in v1:
time: 51.4 us; the launch traced here: 51.1 us
  Pallas kernels  46.3 us (90%)
  local copies, waits for them, and re-layouts  4.2 us (8%)
  between operations  0.64 us (1%)
    pallas_call x1, Pallas kernels, on_device(): pl.pallas_call(functools.partial(kernel, spans, tiles, cores), out_shape=...  46.3 us
    unnamed x1, local copies, waits for them, and re-layouts  1.57 us
    squeeze x1, local copies, waits for them, and re-layouts, on_device(): return (grad, row_values[0, :rows], row_values[1, :rows])  1.26 us

profile of v1, /device:TPU:0, one launch (start us, length us, event | category | flops | bytes accessed | tf_op | source)
XLA Modules:
  0.0 51.1 jit_solution(15767913994720028919)
XLA Ops:
  0.6 0.7 %copy.11 = s32[4,4,16]{2,1,0:T(4,128)S(1)} copy(s32[4,4,16]{2,0,1:T(4,128)} %bitcast.7) | data formatting | bytes 2048 | tf_op jit(solution)/shard_map/transpose | solution.py:325
  1.3 0.7 %reshape.16.request_ref = s32[4,64]{1,0:T(4,128)} reshape(s32[4,4,16]{2,1,0:T(4,128)S(1)} %copy.11) | data formatting | bytes 2048 | tf_op jit(solution)/shard_map/reshape | solution.py:325
  2.0 46.3 %shard_map.103 = (f32[32,1024]{1,0:T(8,128)}, f32[8,128]{1,0:T(8,128)}) custom-call(s32[4,4]{1,0:T(4,128)} %counts_ref.1, bf16[32,1024]{1,0:T(8,128)(2,1)} %student_ref.1, bf16[64,1024]{1,0:T(8,128)(2,1)} %teacher_ref.1, bf16[312,4096]{1,0:T(8,128)(2,1)} %student_head.1, bf16[312,4096]{1,0:T(8,128)(2,1)} %teacher_head.1, s32[1,128]{1,0:T(1,128)} %bitcast.8, ...), custom_call_target="tpu_custom_call" | custom-call | tf_op jit(solution)/shard_map/pallas_call | solution.py:290
  48.3 1.3 %slice_bitcast_fusion = (f32[32]{0:T(128)}, f32[32]{0:T(128)}) fusion(f32[8,128]{1,0:T(8,128)} %get-tuple-element.6), kind=kLoop, calls=%fused_computation | loop fusion | bytes 512 | tf_op jit(solution)/shard_map/squeeze | solution.py:328
  49.6 1.6 %copy.13 = f32[32,1024]{1,0:T(8,128)} copy(f32[32,1024]{1,0:T(8,128)} %get-tuple-element.12) | data formatting | bytes 262144

commit v2 on v1

--- a/solution.py
+++ b/solution.py
@@ -10,14 +10,17 @@
 MESH = pl.DeviceIdType.MESH
 F32 = jnp.float32
 BF16 = jnp.bfloat16
+PIECES = 2
+LATE = (2, 4, 4, 8)
+CROSS = ((1, 1), (1, 3))
 
 
 def kernel(
-    spans, tiles, cores,
+    spans, tiles, cores, pieces,
     counts_ref, student_ref, teacher_ref, student_head, teacher_head, token_ref, request_ref, weight_ref,
     grad_ref, row_ref,
     heads, hidden, slots, arrived, logits, stats, terms, core_in, core_out, tile_in, tile_out, span_in, span_out,
-    head_sem, slot_send, slot_recv, span_send, tile_send, core_send, span_recv, tile_recv, core_recv,
+    head_sem, slot_send, slot_recv, span_send, cross_send, tile_send, core_send, span_recv, tile_recv, core_recv,
     stat_send, stat_recv, gcore_send, gcore_recv, gtile_send, gtile_recv, gspan_send, gspan_recv,
 ):
     group = lax.axis_index("groups")
@@ -30,7 +33,7 @@
     me = v * owners + owner
     rows, width = student_ref.shape
     columns = student_head.shape[0]
-    capacity = request_ref.shape[1] // owners
+    capacity = request_ref.shape[2]
 
     def remote(src, dst, send, recv, at):
         copy = pltpu.make_async_remote_copy(
@@ -48,7 +51,7 @@
     def around(i):
         return lax.rem(me + i, members)
 
-    @pl.loop(1, members)
+    @pl.loop(1, members, unroll=members - 1 if members <= 16 else 1)
     def _(i):
         pl.semaphore_signal(
             pltpu.get_barrier_semaphore(), inc=1, device_id=(group,) + member(around(i)), device_id_type=MESH
@@ -62,13 +65,12 @@
         copy.start()
 
     served = teacher_ref.shape[0]
-    wanted = request_ref[pl.ds(owner, 1), :]
-    pick = (lax.broadcasted_iota(jnp.int32, (served, owners * capacity), 0) == wanted).astype(F32).astype(BF16)
-    slots[...] = (
-        lax.dot_general(pick, teacher_ref[...], (((0,), (0,)), ((), ())), preferred_element_type=F32)
-        .astype(BF16)
-        .reshape(owners, capacity, width)
-    )
+    for o in range(owners):
+        wanted = request_ref[o, pl.ds(owner, 1), :]
+        pick = (lax.broadcasted_iota(jnp.int32, (served, capacity), 0) == wanted).astype(F32).astype(BF16)
+        slots[o] = lax.dot_general(
+            pick, teacher_ref[...], (((0,), (0,)), ((), ())), preferred_element_type=F32
+        ).astype(BF16)
     arrived[owner] = slots[owner]
     hidden[0, v, t, s] = student_ref[...]
 
@@ -83,9 +85,9 @@
             remote(hidden.at[a, w, t, s], hidden.at[a, w, t, s], tile_send.at[a], tile_recv.at[a, w],
                    (v, lax.rem(t + i, tiles), s))
 
-    def to_core(a, w, u):
+    def to_core(a, w):
         for i in range(1, cores):
-            remote(hidden.at[a, w, u, s], hidden.at[a, w, u, s], core_send.at[a], core_recv.at[a, w],
+            remote(hidden.at[a, w, :, s], hidden.at[a, w, :, s], core_send.at[a], core_recv.at[a, w],
                    (v, t, lax.rem(s + i, cores)))
 
     def to_spans(a):
@@ -93,10 +95,20 @@
             remote(hidden.at[a, v, t, s], hidden.at[a, v, t, s], span_send.at[a], span_recv.at[a, v],
                    (lax.rem(v + spans - d, spans), t, s))
 
+    def crosses(a, d):
+        return tiles > 1 and (a, d) in CROSS
+
+    def to_cross(a):
+        for d in range(1, spans):
+            if crosses(a, d):
+                for i in range(1, tiles):
+                    u = lax.rem(t + i, tiles)
+                    remote(hidden.at[a, v, u, s], hidden.at[a, v, u, s], cross_send, tile_recv.at[a, v],
+                           (lax.rem(v + spans - d, spans), t, s))
+
     def start_own(a):
         to_spans(a)
         to_tiles(a, v)
-        to_core(a, v, t)
 
     def take_teacher():
         drain(arrived.at[pl.ds(0, owners - 1)], slot_recv)
@@ -123,15 +135,16 @@
             return
         w = lax.rem(v + d, spans)
         drain(hidden.at[a, w, t, s], span_recv.at[a, w])
-        to_tiles(a, w)
-        to_core(a, w, t)
+        if not crosses(a, d):
+            to_tiles(a, w)
 
     def tile_step(a, d):
         w = lax.rem(v + d, spans)
         if tiles > 1:
             drain(hidden.at[a, w, pl.ds(0, tiles - 1), 0], tile_recv.at[a, w])
-        for i in range(1, tiles):
-            to_core(a, w, lax.rem(t + i, tiles))
+            if d == 0:
+                to_cross(a)
+        to_core(a, w)
 
     def core_step(a, d):
         w = lax.rem(v + d, spans)
@@ -153,15 +166,15 @@
         if d + 1 < spans:
             units.append((0, d + 1))
         units.append((1, d))
-    for i in range(len(units) + 2):
+    for i in range(len(units) + LATE[1]):
         if i < len(units):
             if units[i] == (1, 0):
                 take_teacher()
             span_step(*units[i])
-        if 0 <= i - 1 < len(units):
-            tile_step(*units[i - 1])
-        if 0 <= i - 2:
-            core_step(*units[i - 2])
+        if 0 <= i - LATE[0] < len(units):
+            tile_step(*units[i - LATE[0]])
+        if 0 <= i - LATE[1]:
+            core_step(*units[i - LATE[1]])
 
     student, teacher = logits[0], logits[1]
     ids = me * columns + lax.broadcasted_iota(jnp.int32, student.shape, 0)
@@ -181,7 +194,7 @@
     parts += [jnp.zeros_like(student_top)] * 2
     stats[me] = jnp.concatenate(parts, axis=0)
 
-    @pl.loop(1, members)
+    @pl.loop(1, members, unroll=members - 1 if members <= 16 else 1)
     def _(i):
         remote(stats.at[me], stats.at[me], stat_send, stat_recv, member(around(i)))
 
@@ -204,20 +217,24 @@
     prob = jnp.exp(logits[0] - norm_s)
     slope = (weight_ref[...] * prob * (logits[0] - logits[1] + shift - kl)).astype(BF16)
 
+    cut = width // pieces
+
     def grad_block(d):
-        w = lax.rem(v + d, spans)
+        w = lax.rem(v + d // pieces, spans)
+        from_column = pl.multiple_of(w * width + d % pieces * cut, cut)
         term = lax.dot_general(
             slope,
-            heads[0, :, pl.ds(pl.multiple_of(w * width, width), width)],
+            heads[0, :, pl.ds(from_column, cut)],
             (((0,), (0,)), ((), ())),
             preferred_element_type=F32,
         )
-        terms[d] = term.reshape(tiles, cores, rows, width)
-        core_out[d] = term.astype(BF16).reshape(tiles, cores, rows, width)
+        terms[d] = term.reshape(tiles, cores, rows, cut)
+        sent = term.astype(BF16).reshape(tiles, cores, rows, cut)
+        for k in range(cores):
+            core_out[d, k] = sent[:, k]
         for i in range(1, cores):
             peer = lax.rem(s + i, cores)
-            for u in range(tiles):
-                remote(core_out.at[d, u, peer], core_in.at[d, s, u], gcore_send, gcore_recv.at[d], (v, t, peer))
+            remote(core_out.at[d, peer], core_in.at[d, s], gcore_send, gcore_recv.at[d], (v, t, peer))
 
     def grad_core(d):
         drain(core_in.at[d, pl.ds(0, cores - 1)], gcore_recv.at[d])
@@ -238,43 +255,48 @@
         total = terms[d, t, s]
         for i in range(1, tiles):
             total = total + tile_in[d, lax.rem(t + i, tiles)].astype(F32)
-        if d == 0:
-            grad_ref[...] = total
+        if d < pieces:
+            grad_ref[:, d * cut:(d + 1) * cut] = total
         else:
             span_out[d] = total.astype(BF16)
-            remote(span_out.at[d], span_in.at[d], gspan_send, gspan_recv, (lax.rem(v + d, spans), t, s))
-
-    order = list(range(1, spans)) + [0]
-    for i in range(len(order) + 2):
+            remote(span_out.at[d], span_in.at[d], gspan_send, gspan_recv, (lax.rem(v + d // pieces, spans), t, s))
+
+    order = list(range(pieces, spans * pieces)) + list(range(pieces))
+    for i in range(len(order) + LATE[3]):
         if i < len(order):
             grad_block(order[i])
-        if 0 <= i - 1 < len(order):
-            grad_core(order[i - 1])
-        if 0 <= i - 2:
-            grad_tile(order[i - 2])
+        if 0 <= i - LATE[2] < len(order):
+            grad_core(order[i - LATE[2]])
+        if 0 <= i - LATE[3]:
+            grad_tile(order[i - LATE[3]])
 
     turn = lax.rem(owners - owner, owners) * rows
     row_ref[...] = pltpu.roll(
         jnp.concatenate([kl, ratio] + [jnp.zeros_like(kl)] * 6, axis=0), turn, axis=1
     )
 
-    total = grad_ref[...]
-    drain(span_in.at[pl.ds(1, spans - 1)], gspan_recv)
-    for d in range(1, spans):
-        total = total + span_in[d].astype(F32)
-    grad_ref[...] = total
+    drain(span_in.at[pl.ds(pieces, (spans - 1) * pieces)], gspan_recv)
+    for h in range(pieces):
+        total = grad_ref[:, h * cut:(h + 1) * cut]
+        for d in range(1, spans):
+            total = total + span_in[d * pieces + h].astype(F32)
+        grad_ref[:, h * cut:(h + 1) * cut] = total
 
     drain(slots.at[pl.ds(0, owners - 1)], slot_send)
     for a in range(2):
         drain(hidden.at[a, pl.ds(0, spans - 1), 0, 0], span_send.at[a])
         if tiles > 1:
-            drain(hidden.at[a, :, pl.ds(0, tiles - 1), 0], tile_send.at[a])
+            direct = sum(not crosses(a, d) for d in range(spans))
+            drain(hidden.at[a, pl.ds(0, direct), pl.ds(0, tiles - 1), 0], tile_send.at[a])
         drain(hidden.at[a, :, :, pl.ds(0, cores - 1)], core_send.at[a])
+    crossed = sum(crosses(a, d) for a in range(2) for d in range(1, spans))
+    if crossed:
+        drain(hidden.at[0, pl.ds(0, crossed), pl.ds(0, tiles - 1), 0], cross_send)
     drain(stats.at[pl.ds(0, members - 1)], stat_send)
-    drain(core_out.at[:, :, pl.ds(0, cores - 1)], gcore_send)
+    drain(core_out.at[:, pl.ds(0, cores - 1)], gcore_send)
     if tiles > 1:
         drain(tile_out.at[:, pl.ds(0, tiles - 1)], gtile_send)
-    drain(span_out.at[pl.ds(1, spans - 1)], gspan_send)
+    drain(span_out.at[pl.ds(pieces, (spans - 1) * pieces)], gspan_send)
 
 
 def on_device(mesh, student_hidden, teacher_hidden, student_head, teacher_head, token_ids, requests, counts, kl_weights):
@@ -285,10 +307,11 @@
     columns, features = student_head.shape
     capacity = requests.shape[2]
     total_rows = owners * rows
+    pieces = PIECES if width % (128 * PIECES) == 0 else 1
     vmem = pl.BlockSpec(memory_space=pltpu.VMEM)
     dma = pltpu.SemaphoreType.DMA
     grad, row_values = pl.pallas_call(
-        functools.partial(kernel, spans, tiles, cores),
+        functools.partial(kernel, spans, tiles, cores, pieces),
         out_shape=(
             jax.ShapeDtypeStruct((rows, width), F32),
             jax.ShapeDtypeStruct((8, total_rows), F32),
@@ -305,16 +328,16 @@
             pltpu.VMEM((owners, capacity, width), BF16),
             pltpu.VMEM((2, columns, total_rows), F32),
             pltpu.VMEM((members, 8, total_rows), F32),
-            pltpu.VMEM((spans, tiles, cores, rows, width), F32),
-            pltpu.VMEM((spans, cores, tiles, rows, width), BF16),
-            pltpu.VMEM((spans, tiles, cores, rows, width), BF16),
-            pltpu.VMEM((spans, tiles, rows, width), BF16),
-            pltpu.VMEM((spans, tiles, rows, width), BF16),
-            pltpu.VMEM((spans, rows, width), BF16),
-            pltpu.VMEM((spans, rows, width), BF16),
-            dma((2,)), dma, dma, dma((2,)), dma((2,)), dma((2,)),
+            pltpu.VMEM((spans * pieces, tiles, cores, rows, width // pieces), F32),
+            pltpu.VMEM((spans * pieces, cores, tiles, rows, width // pieces), BF16),
+            pltpu.VMEM((spans * pieces, cores, tiles, rows, width // pieces), BF16),
+            pltpu.VMEM((spans * pieces, tiles, rows, width // pieces), BF16),
+            pltpu.VMEM((spans * pieces, tiles, rows, width // pieces), BF16),
+            pltpu.VMEM((spans * pieces, rows, width // pieces), BF16),
+            pltpu.VMEM((spans * pieces, rows, width // pieces), BF16),
+            dma((2,)), dma, dma, dma((2,)), dma, dma((2,)), dma((2,)),
             dma((2, spans)), dma((2, spans)), dma((2, spans)),
-            dma, dma, dma, dma((spans,)), dma, dma((spans,)), dma, dma,
+            dma, dma, dma, dma((spans * pieces,)), dma, dma((spans * pieces,)), dma, dma,
         ],
         compiler_params=pltpu.CompilerParams(
             collective_id=0, has_side_effects=True, vmem_limit_bytes=56 * 1024 * 1024
@@ -322,7 +345,7 @@
     )(
         counts, student_hidden, teacher_hidden, student_head, teacher_head,
         token_ids.reshape(1, total_rows),
-        requests.transpose(1, 0, 2).reshape(owners, owners * capacity),
+        requests,
         kl_weights.reshape(1, total_rows),
     )
     return grad, row_values[0, :rows], row_values[1, :rows]

time: 51.4 us -> 47.4 us (0.922)
  Pallas kernels: 46.3 us -> 43.7 us
  local copies, waits for them, and re-layouts: 4.2 us -> 2.83 us
    pallas_call x1, Pallas kernels: 46.3 us -> 43.7 us  [on_device(): pl.pallas_call(functools.partial(kernel, spans, tiles, cores, pieces), ou...]
    transpose x1 -> x0, local copies, waits for them, and re-layouts: 0.7 us -> none  [on_device(): requests.transpose(1, 0, 2).reshape(owners, owners * capacity)]
    reshape x1 -> x0, local copies, waits for them, and re-layouts: 0.66 us -> none  [on_device(): requests.transpose(1, 0, 2).reshape(owners, owners * capacity)]
where the time goes in v2:
time: 47.4 us; the launch traced here: 47.2 us
  Pallas kernels  43.7 us (92%)
  local copies, waits for them, and re-layouts  2.83 us (6%)
  between operations  0.64 us (1%)
    pallas_call x1, Pallas kernels, on_device(): pl.pallas_call(functools.partial(kernel, spans, tiles, cores, pieces), ou...  43.7 us
    unnamed x1, local copies, waits for them, and re-layouts  1.57 us
    squeeze x1, local copies, waits for them, and re-layouts, on_device(): return (grad, row_values[0, :rows], row_values[1, :rows])  1.26 us

profile of v2, /device:TPU:0, one launch (start us, length us, event | category | flops | bytes accessed | tf_op | source)
XLA Modules:
  0.0 47.2 jit_solution(11964823518639106851)
XLA Ops:
  0.6 43.7 %shard_map.103 = (f32[32,1024]{1,0:T(8,128)}, f32[8,128]{1,0:T(8,128)}) custom-call(s32[4,4]{1,0:T(4,128)} %counts_ref.1, bf16[32,1024]{1,0:T(8,128)(2,1)} %student_ref.1, bf16[64,1024]{1,0:T(8,128)(2,1)} %teacher_ref.1, bf16[312,4096]{1,0:T(8,128)(2,1)} %student_head.1, bf16[312,4096]{1,0:T(8,128)(2,1)} %teacher_head.1, s32[1,128]{1,0:T(1,128)} %bitcast.6, ...), custom_call_target="tpu_custom_call" | custom-call | tf_op jit(solution)/shard_map/pallas_call | solution.py:313
  44.4 1.3 %slice_bitcast_fusion = (f32[32]{0:T(128)}, f32[32]{0:T(128)}) fusion(f32[8,128]{1,0:T(8,128)} %get-tuple-element.6), kind=kLoop, calls=%fused_computation | loop fusion | bytes 512 | tf_op jit(solution)/shard_map/squeeze | solution.py:351
  45.7 1.6 %copy.12 = f32[32,1024]{1,0:T(8,128)} copy(f32[32,1024]{1,0:T(8,128)} %get-tuple-element.12) | data formatting | bytes 262144

commit v3 on v2

--- a/solution.py
+++ b/solution.py
@@ -107,8 +107,8 @@
                            (lax.rem(v + spans - d, spans), t, s))
 
     def start_own(a):
+        to_tiles(a, v)
         to_spans(a)
-        to_tiles(a, v)
 
     def take_teacher():
         drain(arrived.at[pl.ds(0, owners - 1)], slot_recv)
@@ -297,6 +297,13 @@
     if tiles > 1:
         drain(tile_out.at[:, pl.ds(0, tiles - 1)], gtile_send)
     drain(span_out.at[pl.ds(pieces, (spans - 1) * pieces)], gspan_send)
+
+
+def hand_out(grad_in, row_in, grad_ref, kl_ref, ratio_ref):
+    rows = kl_ref.shape[1]
+    grad_ref[...] = grad_in[...]
+    kl_ref[...] = row_in[0:1, :rows]
+    ratio_ref[...] = row_in[1:2, :rows]
 
 
 def on_device(mesh, student_hidden, teacher_hidden, student_head, teacher_head, token_ids, requests, counts, kl_weights):
@@ -348,7 +355,17 @@
         requests,
         kl_weights.reshape(1, total_rows),
     )
-    return grad, row_values[0, :rows], row_values[1, :rows]
+    grad, kl, log_ratio = pl.pallas_call(
+        hand_out,
+        out_shape=(
+            jax.ShapeDtypeStruct((rows, width), F32),
+            jax.ShapeDtypeStruct((1, rows), F32),
+            jax.ShapeDtypeStruct((1, rows), F32),
+        ),
+        in_specs=[vmem, vmem],
+        out_specs=(vmem, vmem, vmem),
+    )(grad, row_values)
+    return grad, kl.reshape(rows), log_ratio.reshape(rows)
 
 
 def solution(mesh):

time: 47.4 us -> 46.1 us (0.973)
  local copies, waits for them, and re-layouts: 2.83 us -> 0 us
  Pallas kernels: 43.7 us -> 45.3 us
    pallas_call x0 -> x1, Pallas kernels: none -> 1.57 us  [on_device(): pl.pallas_call(hand_out, out_shape=(jax.ShapeDtypeStruct((rows, width), F...]
    unnamed x1 -> x0, local copies, waits for them, and re-layouts: 1.57 us -> none
    squeeze x1 -> x0, local copies, waits for them, and re-layouts: 1.26 us -> none  [on_device(): return (grad, row_values[0, :rows], row_values[1, :rows])]
where the time goes in v3:
time: 46.1 us; the launch traced here: 46 us
  Pallas kernels  45.3 us (98%)
  between operations  0.64 us (1%)
    pallas_call x1, Pallas kernels, on_device(): pl.pallas_call(functools.partial(kernel, spans, tiles, cores, pieces), ou...  43.7 us
    pallas_call x1, Pallas kernels, on_device(): pl.pallas_call(hand_out, out_shape=(jax.ShapeDtypeStruct((rows, width), F...  1.57 us

profile of v3, /device:TPU:0, one launch (start us, length us, event | category | flops | bytes accessed | tf_op | source)
XLA Modules:
  0.0 46.0 jit_solution(5554285887099004719)
XLA Ops:
  0.6 43.7 %shard_map.103 = (f32[32,1024]{1,0:T(8,128)}, f32[8,128]{1,0:T(8,128)}) custom-call(s32[4,4]{1,0:T(4,128)} %counts_ref.1, bf16[32,1024]{1,0:T(8,128)(2,1)} %student_ref.1, bf16[64,1024]{1,0:T(8,128)(2,1)} %teacher_ref.1, bf16[312,4096]{1,0:T(8,128)(2,1)} %student_head.1, bf16[312,4096]{1,0:T(8,128)(2,1)} %teacher_head.1, s32[1,128]{1,0:T(1,128)} %bitcast.4, ...), custom_call_target="tpu_custom_call" | custom-call | tf_op jit(solution)/shard_map/pallas_call | solution.py:320
  44.4 1.6 %shard_map.104 = (f32[32,1024]{1,0:T(8,128)}, f32[1,32]{1,0:T(1,128)}, f32[1,32]{1,0:T(1,128)}) custom-call(f32[32,1024]{1,0:T(8,128)} %get-tuple-element.8.grad_in, f32[8,128]{1,0:T(8,128)} %get-tuple-element.9.row_in), custom_call_target="tpu_custom_call" | custom-call | tf_op jit(solution)/shard_map/pallas_call | solution.py:358

commit v4 on v3

--- a/solution.py
+++ b/solution.py
@@ -12,7 +12,7 @@
 BF16 = jnp.bfloat16
 PIECES = 2
 LATE = (2, 4, 4, 8)
-CROSS = ((1, 1), (1, 3))
+CROSS = ((1, 2), (1, 3))
 
 
 def kernel(

time: 46.1 us -> 46.2 us (level)
  no operation moved by 1% of the time
where the time goes in v4:
time: 46.2 us; the launch traced here: 46 us
  Pallas kernels  45.4 us (98%)
  between operations  0.64 us (1%)
    pallas_call x1, Pallas kernels, on_device(): pl.pallas_call(functools.partial(kernel, spans, tiles, cores, pieces), ou...  43.8 us
    pallas_call x1, Pallas kernels, on_device(): pl.pallas_call(hand_out, out_shape=(jax.ShapeDtypeStruct((rows, width), F...  1.57 us

profile of v4, /device:TPU:0, one launch (start us, length us, event | category | flops | bytes accessed | tf_op | source)
XLA Modules:
  0.0 46.0 jit_solution(16177167545191738820)
XLA Ops:
  0.6 43.8 %shard_map.103 = (f32[32,1024]{1,0:T(8,128)}, f32[8,128]{1,0:T(8,128)}) custom-call(s32[4,4]{1,0:T(4,128)} %counts_ref.1, bf16[32,1024]{1,0:T(8,128)(2,1)} %student_ref.1, bf16[64,1024]{1,0:T(8,128)(2,1)} %teacher_ref.1, bf16[312,4096]{1,0:T(8,128)(2,1)} %student_head.1, bf16[312,4096]{1,0:T(8,128)(2,1)} %teacher_head.1, s32[1,128]{1,0:T(1,128)} %bitcast.4, ...), custom_call_target="tpu_custom_call" | custom-call | tf_op jit(solution)/shard_map/pallas_call | solution.py:320
  44.4 1.6 %shard_map.104 = (f32[32,1024]{1,0:T(8,128)}, f32[1,32]{1,0:T(1,128)}, f32[1,32]{1,0:T(1,128)}) custom-call(f32[32,1024]{1,0:T(8,128)} %get-tuple-element.8.grad_in, f32[8,128]{1,0:T(8,128)} %get-tuple-element.9.row_in), custom_call_target="tpu_custom_call" | custom-call | tf_op jit(solution)/shard_map/pallas_call | solution.py:358
